TPU v7x, 512 devices: a whole 4x4x16 slice. The times are simulated.
512 devices in a mesh: frames: 32 (over y, x, core), atoms: 16 (over z).
Axes of the slice: x: 4, y: 4, z: 16, core: 2. Of those that a mesh axis runs over, the one named last changes fastest.
Arguments:
- frames: float32 [2048, 3, 6144], P('frames', None, 'atoms'), may hold values from -45 to 45, as said below
- reference_structure: float32 [3, 6144], P(None, 'atoms'), may hold values from -15 to 15
Outputs:
- covariance: float32 [3, 6144, 3, 6144], P(None, 'frames', None, 'atoms')
- mean_structure: float32 [3, 6144], P(None, 'atoms')
Inputs may be any that keep to these rules, and one draw needn't show every extreme that they name: `frames`: every frame, once centered, has a cross-covariance with the centered reference_structure of positive determinant whose singular values lie within a factor of 20 of one another.
All inputs are finite; a program needn't handle non-finite values.
Results may differ from a plain program's by a relative error of at most 0.0003.
Values may be sent and summed in bfloat16 or wider, within the bound.
A program may use at most 64 MiB of HBM per device.

v0:
```python
import jax
import jax.numpy as jnp
from jax import lax
from jax.sharding import Mesh
from jax.sharding import PartitionSpec as P

ATOMS = 6144
ITERS = 2
POLAR = 8
FRAMES = ("frames_0", "frames_1", "frames_2")


def copy_for_each(array, axis):
    copies = jnp.broadcast_to(array, (lax.axis_size(axis), *array.shape))
    return lax.all_to_all(copies, axis, split_axis=0, concat_axis=0, tiled=True)


def over_copies(array, axis):
    everything = copy_for_each(array, axis)
    return jnp.sum(everything, axis=0)


def in_one(arrays, axis):
    vector, at, finished = (jnp.concatenate([a.reshape(-1) for a in arrays]), 0, [])
    total = over_copies(vector, axis)
    for a in arrays:
        finished.append(total[at : at + a.size].reshape(a.shape))
        at += a.size
    return tuple(finished)


def in_blocks(array, dim, devices):
    lengths = array.shape
    blocks = array.reshape(*lengths[:dim], devices, lengths[dim] // devices, *lengths[dim + 1 :])
    return jnp.moveaxis(blocks, dim, 0)


def laid_out(blocks, dim):
    blocks = jnp.moveaxis(blocks, 0, dim)
    lengths = blocks.shape
    return blocks.reshape(*lengths[:dim], lengths[dim] * lengths[dim + 1], *lengths[dim + 2 :])


def exchange_in_order(blocks, axes, turns):
    lengths = [lax.axis_size(a) for a in axes]
    blocks = blocks.reshape(*lengths, *blocks.shape[1:])
    for k in turns:
        blocks = lax.all_to_all(blocks, axes[k], split_axis=k, concat_axis=k, tiled=True)
    return blocks.reshape(-1, *blocks.shape[len(axes) :])


def core_and_chips(array, groups, turns, split_dim, concat_dim):
    devices = lax.axis_size(groups[0]) * lax.axis_size(groups[1])
    blocks = in_blocks(array, split_dim, devices)
    return laid_out(exchange_in_order(blocks, groups, turns), concat_dim)


def polar_factor(cross):
    factor = jnp.sqrt(3.0 / jnp.sum(cross * cross, axis=(0, 1)))
    matrix = cross * factor[None, None, :]
    for turn in range(POLAR):
        entries = [[matrix[i, j] for j in range(3)] for i in range(3)]
        cofactor = [
            [
                entries[(i + 1) % 3][(j + 1) % 3] * entries[(i + 2) % 3][(j + 2) % 3]
                - entries[(i + 1) % 3][(j + 2) % 3] * entries[(i + 2) % 3][(j + 1) % 3]
                for j in range(3)
            ]
            for i in range(3)
        ]
        determinant = (
            entries[0][0] * cofactor[0][0]
            + entries[0][1] * cofactor[0][1]
            + entries[0][2] * cofactor[0][2]
        )
        inverse = jnp.stack([jnp.stack(cofactor[i]) for i in range(3)]) / determinant[None, None, :]
        matrix = 0.5 * (matrix + inverse)
    return matrix


def contract_frames(left_rows, right_rows):
    return lax.dot_general(
        left_rows, right_rows, (((0,), (0,)), ((), ())), preferred_element_type=jnp.float32
    )


def body(frames, reference_structure):
    highest = lax.Precision.HIGHEST
    mean_now = reference_structure
    count_all = frames.shape[0] * lax.axis_size(FRAMES)
    for iteration in range(ITERS):
        sum_coords, sum_cross, sum_mean = in_one(
            (
                jnp.sum(frames, axis=2),
                jnp.einsum("fca,da->cdf", frames, mean_now, precision=highest),
                jnp.sum(mean_now, axis=1),
            ),
            "atoms",
        )
        centroid = sum_coords / ATOMS
        cross = sum_cross - centroid.T[:, None, :] * sum_mean[None, :, None]
        shifted = frames - centroid[:, :, None]
        rotation = polar_factor(cross)
        aligned = jnp.einsum("cdf,fca->fda", rotation, shifted, precision=highest)
        mean_now = over_copies(jnp.sum(aligned, axis=0), FRAMES) / count_all
    deviation = (aligned - mean_now[None]).astype(jnp.bfloat16)
    column_atoms = frames.shape[2]
    row_count = column_atoms * lax.axis_size("atoms") // lax.axis_size(FRAMES)
    own_rows = lax.all_gather(deviation, "atoms", axis=2, tiled=True)
    row_panel = core_and_chips(own_rows, (("frames_0", "frames_1"), "frames_2"), (1, 0), 2, 0)
    row_flat = row_panel.reshape(row_panel.shape[0], 3 * row_count)
    piece = lax.all_gather(deviation, FRAMES, axis=0, tiled=True)
    product = contract_frames(row_flat, piece.reshape(piece.shape[0], 3 * column_atoms))
    covariance = (product / count_all).reshape(3, row_count, 3, column_atoms)
    return (covariance, mean_now)


def solution(mesh):
    finer = Mesh(
        mesh.devices.reshape(4, 4, 2, mesh.shape["atoms"]),
        ("frames_0", "frames_1", "frames_2", "atoms"),
    )
    return jax.shard_map(
        body,
        mesh=finer,
        in_specs=(P(FRAMES, None, "atoms"), P(None, "atoms")),
        out_specs=(P(None, FRAMES, None, "atoms"), P(None, "atoms")),
        check_vma=False,
    )
```

profile of v0, /device:TPU:1, one launch (start us, length us, event | category | flops | bytes accessed | tf_op | source)
XLA Modules:
  0.0 279.2 jit_solution(8115866642797572257)
XLA Ops:
  7.2 0.8 reduce_sum.99
  8.1 1.1 reduce_sum.98
  9.1 1.4 convolution_bitcast_fusion.2
  10.6 0.1 reshape.5854
  10.7 0.1 copy.45
  10.8 0.1 reshape.5853
  11.0 0.1 fusion.26
  11.1 27.2 %all_to_all.32 = f32[16,1,771]{2,1,0:T(1,128)S(1)} all-to-all(f32[16,1,771]{2,1,0:T(1,128)S(1)} %broadcast_in_dim.8), channel_id=1, replica_groups=mesh['frames_0'=4,'frames_1'=4,'frames_2'=2,'atoms'=16] {'atoms'}, dimensions={0} | all-to-all | bytes 98688 | tf_op jit(solution)/shard_map/all_to_all | solution.py:15
  38.3 0.1 slice.472
  38.4 0.1 reshape.5855
  38.5 0.1 div.197
  38.6 0.1 copy.48
  38.7 0.1 copy.47
  38.8 0.1 multiply_reduce_fusion.1
  38.9 0.1 fusion.23
  39.0 0.1 fusion.7
  39.2 0.1 fusion.8
  39.4 0.1 fusion.9
  39.5 0.1 fusion.10
  39.7 0.1 fusion.11
  39.9 0.1 fusion.12
  40.0 0.1 fusion.13
  40.2 1.3 convolution_bitcast_fusion.1
  41.6 17.2 %all_to_all.33 = f32[32,3,384]{2,1,0:T(4,128)S(1)} all-to-all(f32[32,3,384]{2,1,0:T(4,128)S(1)} %broadcast_in_dim.9), channel_id=1, replica_groups=mesh['frames_0'=4,'frames_1'=4,'frames_2'=2,'atoms'=16] {'frames_0','fra..., dimensions={0} | all-to-all | bytes 294912 | tf_op jit(solution)/shard_map/all_to_all | solution.py:15
  58.8 0.1 multiply_reduce_fusion.2
  58.9 1.4 convolution_bitcast_fusion
  60.3 0.1 reshape.5856
  60.5 0.1 fusion.25
  60.6 14.2 %all_to_all.34 = f32[16,1,771]{2,1,0:T(1,128)S(1)} all-to-all(f32[16,1,771]{2,1,0:T(1,128)S(1)} %broadcast_in_dim.10), channel_id=1, replica_groups=mesh['frames_0'=4,'frames_1'=4,'frames_2'=2,'atoms'=16] {'atoms'}, dimensions={0} | all-to-all | bytes 98688 | tf_op jit(solution)/shard_map/all_to_all | solution.py:15
  74.9 0.1 slice.547
  74.9 0.1 reshape.5857
  75.0 0.1 div.225
  75.2 0.1 copy.52
  75.2 0.1 copy.51
  75.3 0.1 multiply_reduce_fusion
  75.4 0.1 fusion.24
  75.6 0.1 fusion.14
  75.8 0.1 fusion.15
  75.9 0.1 fusion.16
  76.1 0.1 fusion.17
  76.2 0.1 fusion.18
  76.4 0.1 fusion.19
  76.6 0.1 fusion.20
  76.8 0.1 fusion.21
  76.9 0.1 copy.53
  77.0 0.1 broadcast_subtract_fusion
  77.1 1.1 fusion.33
  78.3 13.2 %all_to_all.35 = f32[32,3,384]{2,1,0:T(4,128)S(1)} all-to-all(f32[32,3,384]{2,1,0:T(4,128)S(1)} %broadcast_in_dim.11), channel_id=1, replica_groups=mesh['frames_0'=4,'frames_1'=4,'frames_2'=2,'atoms'=16] {'frames_0','fra..., dimensions={0} | all-to-all | bytes 294912 | tf_op jit(solution)/shard_map/all_to_all | solution.py:15
  91.5 0.7 subtract_convert_fusion
  92.3 1.6 copy.60
  94.0 64.7 %all-gather.3.cloned.1.call-done = bf16[64,3,6144]{2,1,0:T(4,128)(2,1)} async-done(((bf16[64,3,384]{2,1,0:T(4,128)(2,1)}), bf16[64,3,6144]{2,1,0:T(4,128)(2,1)}) %all-gather.3.cloned.1.call-update) | async-done | bytes 2359312 | tf_op jit(solution)/shard_map/all_gather | solution.py:109
  158.7 3.6 %copy.56 = bf16[64,3,6144]{2,0,1:T(8,128)(2,1)S(1)} copy(bf16[64,3,6144]{2,1,0:T(4,128)(2,1)} %all-gather.3.cloned.1.call-done) | data formatting | bytes 4718592 | tf_op jit(solution)/shard_map/all_gather | solution.py:109
  162.3 4.6 %reshape.5858 = bf16[64,3,32,192]{3,2,0,1:T(8,128)(2,1)} reshape(bf16[64,3,6144]{2,0,1:T(8,128)(2,1)S(1)} %copy.56) | data formatting | bytes 4718592 | tf_op jit(solution)/shard_map/reshape | solution.py:34
  166.8 4.3 %reshape.5859 = bf16[16,2,64,3,192]{4,1,0,2,3:T(2,128)(2,1)S(1)} reshape(bf16[32,64,3,192]{3,0,1,2:T(8,128)(2,1)} %bitcast.395) | data formatting | bytes 4718592 | tf_op jit(solution)/shard_map/reshape | solution.py:46
  171.1 1.8 copy.57
  172.9 15.7 %all_to_all.36 = bf16[16,2,64,3,192]{4,2,3,0,1:T(8,128)(2,1)S(1)} all-to-all(bf16[16,2,64,3,192]{4,2,3,0,1:T(8,128)(2,1)S(1)} %copy.57), channel_id=1, replica_groups=mesh['frames_0'=4,'frames_1'=4,'frames_2'=2,'atoms'=16] {'frames_2'}, dimensions={1} | all-to-all | bytes 4718592 | tf_op jit(solution)/shard_map/all_to_all | solution.py:48
  188.6 0.4 copy.58
  189.0 50.7 %all_to_all.37 = bf16[16,2,64,3,192]{4,2,3,1,0:T(8,128)(2,1)S(1)} all-to-all(bf16[16,2,64,3,192]{4,2,3,1,0:T(8,128)(2,1)S(1)} %copy.58), channel_id=1, replica_groups=mesh['frames_0'=4,'frames_1'=4,'frames_2'=2,'atoms'=16] {'frames_0','fra..., dimensions={0} | all-to-all | bytes 4718592 | tf_op jit(solution)/shard_map/all_to_all | solution.py:48
  239.6 5.0 %copy.59 = bf16[16,2,64,3,192]{4,3,2,1,0:T(4,128)(2,1)} copy(bf16[16,2,64,3,192]{4,2,3,1,0:T(8,128)(2,1)S(1)} %all_to_all.37) | data formatting | bytes 4718592 | tf_op jit(solution)/shard_map/all_to_all | solution.py:48
  244.7 8.0 %reshape_reshape_reshape.3 = bf16[2048,576]{1,0:T(8,128)(2,1)S(1)} reshape(bf16[16,2,64,3,192]{4,3,2,1,0:T(4,128)(2,1)} %copy.59) | data formatting | bytes 4718592 | tf_op jit(solution)/shard_map/reshape;reshape;reshape | solution.py:111
  252.8 6.7 %copy.61 = bf16[2048,3,384]{0,2,1:T(8,128)(2,1)} copy(bf16[2048,3,384]{2,0,1:T(8,128)(2,1)} %all-gather.5.cloned.1.call-done) | data formatting | bytes 9437184 | tf_op jit(solution)/shard_map/all_gather | solution.py:112
  259.5 7.4 %convolution_multiply_fusion = f32[576,1152]{1,0:T(8,128)} fusion(bf16[2048,576]{1,0:T(8,128)(2,1)S(1)} %reshape_reshape_reshape.3, bf16[2048,1152]{0,1:T(8,128)(2,1)} %bitcast.396), kind=kOutput, calls=%fused_computation | convolution fusion | flops 2718572544 | bytes 9732096 | tf_op jit(solution)/shard_map/dot_general | solution.py:82
  266.9 3.7 %reshape.5861 = f32[3,192,3,384]{3,2,1,0:T(4,128)S(1)} reshape(f32[576,1152]{1,0:T(8,128)} %convolution_multiply_fusion) | data formatting | bytes 5308416 | tf_op jit(solution)/shard_map/reshape | solution.py:114
  270.7 1.7 copy.62
  (103 shorter events, 1.4 us)
Async XLA Ops:
  7.2 69.9 %copy-start = (f32[64,3,384]{2,0,1:T(8,128)S(1)}, f32[64,3,384]{2,0,1:T(8,128)}, u32[]{:S(2)}) copy-start(f32[64,3,384]{2,0,1:T(8,128)} %param.2) | copy-start | bytes 884740
  7.2 151.5 %all-gather.3.cloned.1.call-start = ((), (), s32[]{:S(2)}) async-start(), calls=%async_computation.6 | async-start | bytes 3342336 | tf_op jit(solution)/shard_map/all_gather | solution.py:109
  91.5 70.7 %copy-start.1 = (f32[3,384]{1,0:T(4,128)}, f32[3,384]{1,0:T(4,128)S(1)}, u32[]{:S(2)}) copy-start(f32[3,384]{1,0:T(4,128)S(1)} %broadcast_multiply_fusion) | copy-start | bytes 13828
  92.3 160.4 %all-gather.5.cloned.1.call-start = ((), (), s32[]{:S(2)}) async-start(), calls=%async_computation.7 | async-start | bytes 4866048 | tf_op jit(solution)/shard_map/all_gather | solution.py:112
Sparse Core Ops, SparseCore 0:
  92.4 66.1 all-gather.2
  161.8 84.1 all-gather.4
where the time goes:
time: 282 us; the launch traced here: 279 us
  blocking collectives  138 us (49%)
  waiting for transfers between devices  64.7 us (23%)
  local copies, waits for them, and re-layouts  43.1 us (15%)
  between operations  14.7 us (5%)
  matrix products  12.7 us (5%)
  other arithmetic  5.79 us (2%)
    all_to_all x4, blocking collectives, copy_for_each(): return lax.all_to_all(copies, axis, split_axis=0, concat_axis=0, tiled=True)  71.7 us
    all_to_all x2, blocking collectives, exchange_in_order(): lax.all_to_all(blocks, axes[k], split_axis=k, concat_axis=k, tiled=True)  66.4 us
    all_gather x1, waiting for transfers between devices, body(): own_rows = lax.all_gather(deviation, 'atoms', axis=2, tiled=True)  64.7 us
    another operation x1, local copies, waits for them, and re-layouts, body(): row_flat = row_panel.reshape(row_panel.shape[0], 3 * row_count)  8.03 us
    dot_general x1, matrix products, contract_frames(): lax.dot_general(left_rows, right_rows, (((0,), (0,)), ((), ())), preferre...  7.42 us
    all_gather x1, local copies, waits for them, and re-layouts, body(): piece = lax.all_gather(deviation, FRAMES, axis=0, tiled=True)  6.75 us
    reshape x2, local copies, waits for them, and re-layouts, exchange_in_order(): blocks = blocks.reshape(*lengths, *blocks.shape[1:])  6.04 us
  transfers between devices with their start and end apart: 2, of which 1 were waited for; matrix products, arithmetic and copies ran while one was open for 10% of the time, Pallas kernels for 0%

commit v1 on v0

v1 whole, which is shorter than its diff:
```python
import jax
import jax.numpy as jnp
from jax import lax
from jax.experimental import pallas as pl
from jax.experimental.pallas import tpu as pltpu
from jax.sharding import PartitionSpec as P

ATOMS = 6144
FRAMES = 2048
POLAR = 8
F = 64
A = 384
W = 3 * A
NZ = 16
NP = 32
H = F // 2
MESH = pl.DeviceIdType.MESH
HIGHEST = lax.Precision.HIGHEST


def polar_factor(cross):
    square = sum(cross[i][j] * cross[i][j] for i in range(3) for j in range(3))
    factor = jnp.sqrt(3.0 / square)
    flat = tuple(cross[i][j] * factor for i in range(3) for j in range(3))

    def turn(_, flat):
        e = [flat[0:3], flat[3:6], flat[6:9]]
        cof = [
            [
                e[(i + 1) % 3][(j + 1) % 3] * e[(i + 2) % 3][(j + 2) % 3]
                - e[(i + 1) % 3][(j + 2) % 3] * e[(i + 2) % 3][(j + 1) % 3]
                for j in range(3)
            ]
            for i in range(3)
        ]
        det = e[0][0] * cof[0][0] + e[0][1] * cof[0][1] + e[0][2] * cof[0][2]
        half = 0.5 / det
        return tuple(0.5 * e[i][j] + cof[i][j] * half for i in range(3) for j in range(3))

    flat = lax.fori_loop(0, POLAR, turn, flat)
    return [flat[0:3], flat[3:6], flat[6:9]]


def kernel(
    frames_ref, ref_ref, cov_ref, mean_ref,
    fa, aug, w, tile, rt, al, zbuf, pbuf, col, row, acc,
    z_send, z_recv, p_send, p_recv,
    a_send, a_recv, b_send, b_recv, cs_send, cs_recv,
    swap_send, swap_recv, r_send, r_recv, rs_send, rs_recv,
):
    me = lax.axis_index("frames")
    z = lax.axis_index("atoms")
    c = me // 2
    k = me % 2
    y = c // 4
    x = c % 4
    pa = x + k * (y - x)
    pb = y + k * (x - y)
    partner = (z * 2 + k, c)
    sibling = (c * 2 + 1 - k, z)

    barrier = pltpu.get_barrier_semaphore()

    def greet_z(j, _):
        pl.semaphore_signal(barrier, inc=1, device_id=(me, (z + j) % NZ), device_id_type=MESH)
        return 0

    def greet_p(j, _):
        pl.semaphore_signal(barrier, inc=1, device_id=((me + j) % NP, z), device_id_type=MESH)
        return 0

    lax.fori_loop(1, NZ, greet_z, 0)
    lax.fori_loop(1, NP, greet_p, 0)

    @pl.when(c != z)
    def _():
        pl.semaphore_signal(barrier, inc=1, device_id=partner, device_id_type=MESH)

    fa[0:F, :] = frames_ref[:, 0, :]
    fa[F : 2 * F, :] = frames_ref[:, 2, :]
    fa[2 * F : 3 * F, :] = frames_ref[:, 1, :]
    fa[3 * F : 4 * F, :] = jnp.ones((F, A), jnp.float32)
    aug[...] = jnp.zeros((16, A), jnp.float32)
    aug[3:4, :] = jnp.ones((1, A), jnp.float32)
    aug[15:16, :] = jnp.ones((1, A), jnp.float32)
    w[...] = jnp.zeros((8, 4 * F), jnp.float32)
    rt[...] = jnp.zeros((16, 2 * F), jnp.float32)
    acc[...] = jnp.zeros((3, 256, W), jnp.float32)
    low = lax.broadcasted_iota(jnp.int32, (1, 2 * F), 1) < F

    def local_sums():
        nt = (((1,), (1,)), ((), ()))
        first = lax.dot_general(
            aug[0:8, :], fa[0 : 2 * F, :], nt, precision=HIGHEST, preferred_element_type=jnp.float32
        )
        second = lax.dot_general(
            aug[8:16, :], fa[2 * F : 4 * F, :], nt, precision=HIGHEST, preferred_element_type=jnp.float32
        )
        return first + second

    mean_now = ref_ref[...]
    for p in range(2):
        aug[0:3, :] = mean_now
        aug[12:15, :] = mean_now
        zbuf[p, z] = local_sums()
        if p == 0:
            pl.semaphore_wait(barrier, NZ + NP - 2 + jnp.where(c != z, 1, 0))

        def z_copy(j):
            return pltpu.make_async_remote_copy(
                zbuf.at[p, z], zbuf.at[p, z], z_send.at[p, j], z_recv.at[p, z],
                device_id=(me, (z + j) % NZ), device_id_type=MESH,
            )

        def z_start(j, _):
            z_copy(j).start()
            return 0

        def z_wait(j, _):
            other = (z + j) % NZ
            pltpu.make_async_remote_copy(
                zbuf.at[p, other], zbuf.at[p, other], z_send.at[p, j], z_recv.at[p, other],
                device_id=(me, other), device_id_type=MESH,
            ).wait_recv()
            return 0

        lax.fori_loop(1, NZ, z_start, 0)
        lax.fori_loop(1, NZ, z_wait, 0)
        total = zbuf[p, 0]
        for i in range(1, NZ):
            total = total + zbuf[p, i]
        tile[0:8, :] = total
        tile[8:16, :] = pltpu.roll(total, F, 1)
        centroid = [tile[r : r + 1, :] / ATOMS for r in (3, 7, 11)]
        cross = [
            [tile[4 * i + d : 4 * i + d + 1, :] - centroid[i] * tile[12 + d : 13 + d, :] for d in range(3)]
            for i in range(3)
        ]
        rotation = polar_factor(cross)
        for d in range(3):
            back = -(
                rotation[0][d] * centroid[0] + rotation[1][d] * centroid[1] + rotation[2][d] * centroid[2]
            )
            w[d : d + 1, 0 : 2 * F] = jnp.where(low, rotation[0][d], pltpu.roll(rotation[2][d], F, 1))
            w[d : d + 1, 2 * F : 4 * F] = jnp.where(low, rotation[1][d], pltpu.roll(back, F, 1))
        part = lax.dot_general(
            w[...], fa[...], (((1,), (0,)), ((), ())), precision=HIGHEST, preferred_element_type=jnp.float32
        )
        pbuf[p, me] = part[0:4, :]

        def p_start(j, _):
            pltpu.make_async_remote_copy(
                pbuf.at[p, me], pbuf.at[p, me], p_send.at[p, j], p_recv.at[p, me],
                device_id=((me + j) % NP, z), device_id_type=MESH,
            ).start()
            return 0

        def p_wait(j, _):
            other = (me + j) % NP
            pltpu.make_async_remote_copy(
                pbuf.at[p, other], pbuf.at[p, other], p_send.at[p, j], p_recv.at[p, other],
                device_id=(other, z), device_id_type=MESH,
            ).wait_recv()
            return 0

        lax.fori_loop(1, NP, p_start, 0)
        if p == 1:
            for i in range(3):
                for d in range(3):
                    rt[3 * i + d : 3 * i + d + 1, :] = rotation[i][d]
                rt[9 + i : 10 + i, :] = centroid[i]
            columns = jnp.transpose(rt[...])[0:F, :]
            shifted = [
                fa[at : at + F, :] - columns[:, 9 + i : 10 + i] for i, at in enumerate((0, 2 * F, F))
            ]
            for d in range(3):
                al[d] = sum(columns[:, 3 * i + d : 3 * i + d + 1] * shifted[i] for i in range(3))
        lax.fori_loop(1, NP, p_wait, 0)
        summed = pbuf[p, 0]
        for i in range(1, NP):
            summed = summed + pbuf[p, i]
        mean_now = summed[0:3, :] / FRAMES

    mean_ref[...] = mean_now
    for d in range(3):
        col[c, k, :, d * A : (d + 1) * A] = (al[d] - mean_now[d : d + 1, :]).astype(jnp.bfloat16)

    @pl.when(c == z)
    def _():
        row[z, k] = col[c, k]

    def copy(src, dst, send, recv, device):
        return pltpu.make_async_remote_copy(src, dst, send, recv, device_id=device, device_id_type=MESH)

    def swap(slot):
        return copy(col.at[c, k], row.at[slot, k], swap_send, swap_recv, partner)

    @pl.when(c != z)
    def _():
        swap(c).start()

    def chip(oa, ob):
        qa, qb = (pa + oa) % 4, (pb + ob) % 4
        return (qb + k * (qa - qb)) * 4 + qa + k * (qb - qa)

    def at(oa, ob):
        return (chip(oa, ob) * 2 + k, z)

    def part_of(slot, half):
        if half is None:
            return col.at[slot, k]
        return col.at[slot, k, half * H : (half + 1) * H]

    HALF = (None, None, 0, 1)
    TOWARD = (1, 3, 1, 3)

    def a_copy(kind, slot):
        r = part_of(slot, HALF[kind])
        return copy(r, r, a_send.at[kind], a_recv.at[kind], at(TOWARD[kind], 0))

    def b_copy(oa, kind, slot):
        r = part_of(slot, HALF[kind])
        return copy(r, r, b_send.at[oa, kind], b_recv.at[oa, kind], at(0, TOWARD[kind]))

    def col_sibling(slot, core):
        r = col.at[slot, core]
        return copy(r, r, cs_send.at[slot], cs_recv.at[slot], sibling)

    def have(oa):
        slot = chip(oa, 0)
        b_copy(oa, 0, slot).start()
        b_copy(oa, 1, slot).start()
        col_sibling(slot, k).start()

    def b_pass(oa):
        before, after = chip(oa, 3), chip(oa, 1)
        b_copy(oa, 0, before).wait_recv()
        b_copy(oa, 2, before).start()
        col_sibling(before, k).start()
        b_copy(oa, 1, after).wait_recv()
        b_copy(oa, 3, after).start()
        col_sibling(after, k).start()

    def b_end(oa):
        slot = chip(oa, 2)
        b_copy(oa, 2, slot).wait_recv()
        b_copy(oa, 3, slot).wait_recv()
        col_sibling(slot, k).start()

    right, left = (me, (z + 1) % NZ), (me, (z + NZ - 1) % NZ)

    def r_copy(way, step, h, slot):
        r = row.at[slot, k, h * H : (h + 1) * H]
        return copy(r, r, r_send.at[way, step, h], r_recv.at[way, step, h], right if way == 0 else left)

    def row_sibling(offset, core):
        r = row.at[(z + offset) % NZ, core]
        return copy(r, r, rs_send.at[offset], rs_recv.at[offset], sibling)

    def z_step(s, last=False):
        before, after = (z + NZ - s) % NZ, (z + s) % NZ
        for h in range(2):
            r_copy(0, s - 1, h, before).wait_recv()
            if not last or h == 0:
                r_copy(0, s, h, before).start()
            r_copy(1, s - 1, h, after).wait_recv()
            if not last or h == 1:
                r_copy(1, s, h, after).start()
        row_sibling(NZ - s, k).start()
        row_sibling(s, k).start()

    def accumulate(one, two):
        def component(d, _):
            lanes = pl.ds(pl.multiple_of(d * A + k * 128, 128), 256)
            lhs = jnp.concatenate(
                [row[one, 0, :, lanes], row[one, 1, :, lanes], row[two, 0, :, lanes], row[two, 1, :, lanes]], axis=0
            )
            rhs = jnp.concatenate([col[one, 0], col[one, 1], col[two, 0], col[two, 1]], axis=0)
            acc[d] += lax.dot_general(
                lhs, rhs, (((0,), (0,)), ((), ())), preferred_element_type=jnp.float32
            )
            return 0

        lax.fori_loop(0, 3, component, 0)

    def z_compute(s):
        row_sibling(s, 1 - k).wait_recv()
        row_sibling(NZ - s, 1 - k).wait_recv()
        accumulate((z + NZ - s) % NZ, (z + s) % NZ)

    a_copy(0, c).start()
    a_copy(1, c).start()
    have(0)
    a_copy(0, chip(3, 0)).wait_recv()
    a_copy(2, chip(3, 0)).start()
    have(3)
    a_copy(1, chip(1, 0)).wait_recv()
    a_copy(3, chip(1, 0)).start()
    have(1)

    @pl.when(c != z)
    def _():
        swap(z).wait_recv()

    for h in range(2):
        r_copy(0, 0, h, z).start()
        r_copy(1, 0, h, z).start()
    row_sibling(0, k).start()
    b_pass(0)
    a_copy(2, chip(2, 0)).wait_recv()
    a_copy(3, chip(2, 0)).wait_recv()
    have(2)
    b_pass(3)
    z_step(1)
    b_pass(1)
    b_pass(2)
    z_step(2)
    for oa in (0, 3, 1, 2):
        b_end(oa)

    def col_wait(q, _):
        col_sibling(q, 1 - k).wait_recv()
        return 0

    def compute(s, _):
        z_compute(s)
        return 0

    def middle(s, _):
        z_step(s)
        z_compute(s - 1)
        return 0

    z_step(3)
    lax.fori_loop(0, NZ, col_wait, 0)
    lax.fori_loop(1, 3, compute, 0)
    lax.fori_loop(4, 7, middle, 0)
    z_step(7, last=True)
    lax.fori_loop(6, 8, compute, 0)
    far = (z + NZ // 2) % NZ
    r_copy(0, 7, 0, far).wait_recv()
    r_copy(1, 7, 1, far).wait_recv()
    row_sibling(NZ // 2, k).start()
    row_sibling(0, 1 - k).wait_recv()
    row_sibling(NZ // 2, 1 - k).wait_recv()
    accumulate(z, far)
    for d in range(3):
        cov_ref[d] = acc[d, pl.ds(pl.multiple_of(k * F, F), 192), :] * (1.0 / FRAMES)

    def a_sent(j, _):
        for p in range(2):
            copy(zbuf.at[p, z], zbuf.at[p, z], z_send.at[p, j], z_recv.at[p, z], (me, (z + j) % NZ)).wait_send()
        return 0

    def p_sent(j, _):
        for p in range(2):
            copy(pbuf.at[p, me], pbuf.at[p, me], p_send.at[p, j], p_recv.at[p, me], ((me + j) % NP, z)).wait_send()
        return 0

    def slot_sent(q, _):
        col_sibling(q, k).wait_send()
        row_sibling(q, k).wait_send()
        return 0

    def b_sent(oa, _):
        for kind in range(4):
            b_copy(oa, kind, c).wait_send()
        return 0

    def r_sent(s, _):
        for way in range(2):
            for h in range(2):
                r_copy(way, s, h, z).wait_send()
        return 0

    lax.fori_loop(1, NZ, a_sent, 0)
    lax.fori_loop(1, NP, p_sent, 0)
    lax.fori_loop(0, NZ, slot_sent, 0)
    for kind in range(4):
        a_copy(kind, c).wait_send()
    lax.fori_loop(0, 4, b_sent, 0)
    lax.fori_loop(0, NZ // 2 - 1, r_sent, 0)
    r_copy(0, 7, 0, z).wait_send()
    r_copy(1, 7, 1, z).wait_send()

    @pl.when(c != z)
    def _():
        swap(c).wait_send()


def body(frames, reference_structure):
    dma = pltpu.SemaphoreType.DMA
    vmem = pl.BlockSpec(memory_space=pltpu.VMEM)
    covariance, mean = pl.pallas_call(
        kernel,
        out_shape=(
            jax.ShapeDtypeStruct((3, A // 2, W), jnp.float32),
            jax.ShapeDtypeStruct((3, A), jnp.float32),
        ),
        in_specs=[vmem, vmem],
        out_specs=(vmem, vmem),
        scratch_shapes=[
            pltpu.VMEM((4 * F, A), jnp.float32),
            pltpu.VMEM((16, A), jnp.float32),
            pltpu.VMEM((8, 4 * F), jnp.float32),
            pltpu.VMEM((16, 2 * F), jnp.float32),
            pltpu.VMEM((16, 2 * F), jnp.float32),
            pltpu.VMEM((3, F, A), jnp.float32),
            pltpu.VMEM((2, NZ, 8, 2 * F), jnp.float32),
            pltpu.VMEM((2, NP, 4, A), jnp.float32),
            pltpu.VMEM((NZ, 2, F, W), jnp.bfloat16),
            pltpu.VMEM((NZ, 2, F, W), jnp.bfloat16),
            pltpu.VMEM((3, 256, W), jnp.float32),
            dma((2, NZ)), dma((2, NZ)), dma((2, NP)), dma((2, NP)),
            dma((4,)), dma((4,)), dma((4, 4)), dma((4, 4)), dma((NZ,)), dma((NZ,)),
            dma, dma, dma((2, 8, 2)), dma((2, 8, 2)), dma((NZ,)), dma((NZ,)),
        ],
        compiler_params=pltpu.CompilerParams(
            collective_id=0, has_side_effects=True, vmem_limit_bytes=44 * 1024 * 1024
        ),
        cost_estimate=pl.CostEstimate(flops=3_000_000_000, bytes_accessed=8_000_000, transcendentals=0),
    )(frames, reference_structure)
    return covariance.reshape(3, A // 2, 3, A), mean


def solution(mesh):
    return jax.shard_map(
        body,
        mesh=mesh,
        in_specs=(P("frames", None, "atoms"), P(None, "atoms")),
        out_specs=(P(None, "frames", None, "atoms"), P(None, "atoms")),
        check_vma=False,
    )
```

time: 282 us -> 126 us (0.45)
  blocking collectives: 138 us -> 0 us
  Pallas kernels: 0 us -> 121 us
  waiting for transfers between devices: 64.7 us -> 0 us
  local copies, waits for them, and re-layouts: 43.1 us -> 4.16 us
  between operations: 14.7 us -> 0.65 us
  matrix products: 12.7 us -> 0 us
  other arithmetic: 5.79 us -> 0 us
    all_to_all x6 -> x0, blocking collectives: 138 us -> none  [the longest x4 71.7 us: copy_for_each(): return lax.all_to_all(copies, axis, split_axis=0, concat_axis=0, tiled=True)]
    pallas_call x0 -> x1, Pallas kernels: none -> 121 us  [body(): pl.pallas_call(kernel, out_shape=(jax.ShapeDtypeStruct((3, A // 2, W), jn...]
    all_gather x2 -> x0, waiting for transfers between devices: 64.7 us -> none  [the longest x1 64.7 us: body(): own_rows = lax.all_gather(deviation, 'atoms', axis=2, tiled=True)]
    reshape x9 -> x1, local copies, waits for them, and re-layouts: 14.9 us -> 1.72 us  [body(): return (covariance.reshape(3, A // 2, 3, A), mean)]
    dot_general x5 -> x0, matrix products: 12.7 us -> none  [the longest x1 7.42 us: contract_frames(): lax.dot_general(left_rows, right_rows, (((0,), (0,)), ((), ())), preferre...]
    all_gather x2 -> x0, local copies, waits for them, and re-layouts: 10.3 us -> none  [the longest x1 6.75 us: body(): piece = lax.all_gather(deviation, FRAMES, axis=0, tiled=True)]
    another operation x1 -> x0, local copies, waits for them, and re-layouts: 8.03 us -> none  [body(): row_flat = row_panel.reshape(row_panel.shape[0], 3 * row_count)]
    all_to_all x2 -> x0, local copies, waits for them, and re-layouts: 5.44 us -> none  [exchange_in_order(): lax.all_to_all(blocks, axes[k], split_axis=k, concat_axis=k, tiled=True)]
  transfers between devices with their start and end apart: 2 -> 0, of which waited for: 1 -> 0; matrix products, arithmetic and copies ran while one was open for 10% -> 0% of each run, Pallas kernels for 0% -> 0%
where the time goes in v1:
time: 126 us; the launch traced here: 125 us
  Pallas kernels  121 us (96%)
  local copies, waits for them, and re-layouts  4.16 us (3%)
    pallas_call x1, Pallas kernels, body(): pl.pallas_call(kernel, out_shape=(jax.ShapeDtypeStruct((3, A // 2, W), jn...  121 us

profile of v1, /device:TPU:1, one launch (start us, length us, event | category | flops | bytes accessed | tf_op | source)
XLA Modules:
  0.0 125.4 jit_solution(12857489124010767056)
XLA Ops:
  0.6 1.2 copy.6.frames_ref
  1.8 0.0 copy-start
  1.8 0.7 copy-done
  2.5 120.6 %shard_map.41 = (f32[3,192,1152]{2,1,0:T(8,128)S(1)}, f32[3,384]{1,0:T(4,128)S(1)}) custom-call(f32[64,3,384]{2,1,0:T(4,128)S(1)} %copy.6.frames_ref, f32[3,384]{1,0:T(4,128)S(1)} %copy-done), custom_call_target="tpu_custom_call" | custom-call | flops 3000000000 | bytes 8000000 | tf_op jit(solution)/shard_map/pallas_call | solution.py:394
  123.1 1.7 %copy.10 = f32[3,24,3,8,384]{4,3,1,2,0:T(8,128)} copy(f32[3,24,3,8,384]{4,3,2,1,0:T(8,128)S(1)} %bitcast.4) | data formatting | bytes 5308416 | tf_op jit(solution)/shard_map/reshape | solution.py:423
  124.8 0.6 copy.12
Async XLA Ops:
  1.8 0.7 copy-start

commit v2 on v1

--- a/solution.py
+++ b/solution.py
@@ -14,6 +14,8 @@
 NZ = 16
 NP = 32
 H = F // 2
+CH = 4
+Q = F // CH
 MESH = pl.DeviceIdType.MESH
 HIGHEST = lax.Precision.HIGHEST
 
@@ -43,10 +45,10 @@
 
 def kernel(
     frames_ref, ref_ref, cov_ref, mean_ref,
-    fa, aug, w, tile, rt, al, zbuf, pbuf, col, row, acc,
+    fa, aug, w, tile, rt, al, zbuf, pbuf, mid, col, row, acc,
     z_send, z_recv, p_send, p_recv,
     a_send, a_recv, b_send, b_recv, cs_send, cs_recv,
-    swap_send, swap_recv, r_send, r_recv, rs_send, rs_recv,
+    l_send, l_recv, r_send, r_recv, rs_send, rs_recv,
 ):
     me = lax.axis_index("frames")
     z = lax.axis_index("atoms")
@@ -56,29 +58,39 @@
     x = c % 4
     pa = x + k * (y - x)
     pb = y + k * (x - y)
-    partner = (z * 2 + k, c)
     sibling = (c * 2 + 1 - k, z)
 
+    def copy(src, dst, send, recv, device):
+        return pltpu.make_async_remote_copy(src, dst, send, recv, device_id=device, device_id_type=MESH)
+
+    def z_other(i):
+        return (z + 8 + ((i + 1) // 2) * (2 * (i % 2) - 1)) % NZ
+
+    def p_other(i):
+        return (((y + i // 8 + 2) % 4) * 4 + (x + i // 2 + 2) % 4) * 2 + (k + i) % 2
+
+    def over_z(act):
+        def turn(i, _):
+            act(i, z_other(i))
+            return 0
+
+        lax.fori_loop(0, NZ - 1, turn, 0)
+
+    def over_p(act):
+        def turn(i, _):
+            act(i, p_other(i))
+            return 0
+
+        lax.fori_loop(0, 20, turn, 0)
+        lax.fori_loop(21, NP, turn, 0)
+
     barrier = pltpu.get_barrier_semaphore()
-
-    def greet_z(j, _):
-        pl.semaphore_signal(barrier, inc=1, device_id=(me, (z + j) % NZ), device_id_type=MESH)
-        return 0
-
-    def greet_p(j, _):
-        pl.semaphore_signal(barrier, inc=1, device_id=((me + j) % NP, z), device_id_type=MESH)
-        return 0
-
-    lax.fori_loop(1, NZ, greet_z, 0)
-    lax.fori_loop(1, NP, greet_p, 0)
-
-    @pl.when(c != z)
-    def _():
-        pl.semaphore_signal(barrier, inc=1, device_id=partner, device_id_type=MESH)
-
-    fa[0:F, :] = frames_ref[:, 0, :]
-    fa[F : 2 * F, :] = frames_ref[:, 2, :]
-    fa[2 * F : 3 * F, :] = frames_ref[:, 1, :]
+    over_z(lambda i, o: pl.semaphore_signal(barrier, inc=1, device_id=(me, o), device_id_type=MESH))
+    over_p(lambda i, o: pl.semaphore_signal(barrier, inc=1, device_id=(o, z), device_id_type=MESH))
+
+    fa[0:F, :] = frames_ref[0]
+    fa[F : 2 * F, :] = frames_ref[2]
+    fa[2 * F : 3 * F, :] = frames_ref[1]
     fa[3 * F : 4 * F, :] = jnp.ones((F, A), jnp.float32)
     aug[...] = jnp.zeros((16, A), jnp.float32)
     aug[3:4, :] = jnp.ones((1, A), jnp.float32)
@@ -104,28 +116,13 @@
         aug[12:15, :] = mean_now
         zbuf[p, z] = local_sums()
         if p == 0:
-            pl.semaphore_wait(barrier, NZ + NP - 2 + jnp.where(c != z, 1, 0))
-
-        def z_copy(j):
-            return pltpu.make_async_remote_copy(
-                zbuf.at[p, z], zbuf.at[p, z], z_send.at[p, j], z_recv.at[p, z],
-                device_id=(me, (z + j) % NZ), device_id_type=MESH,
-            )
-
-        def z_start(j, _):
-            z_copy(j).start()
-            return 0
-
-        def z_wait(j, _):
-            other = (z + j) % NZ
-            pltpu.make_async_remote_copy(
-                zbuf.at[p, other], zbuf.at[p, other], z_send.at[p, j], z_recv.at[p, other],
-                device_id=(me, other), device_id_type=MESH,
-            ).wait_recv()
-            return 0
-
-        lax.fori_loop(1, NZ, z_start, 0)
-        lax.fori_loop(1, NZ, z_wait, 0)
+            pl.semaphore_wait(barrier, NZ + NP - 2)
+
+        def z_copy(i, o, slot):
+            return copy(zbuf.at[p, slot], zbuf.at[p, slot], z_send.at[p, i], z_recv.at[p, slot], (me, o))
+
+        over_z(lambda i, o: z_copy(i, o, z).start())
+        over_z(lambda i, o: z_copy(i, o, o).wait_recv())
         total = zbuf[p, 0]
         for i in range(1, NZ):
             total = total + zbuf[p, i]
@@ -148,34 +145,20 @@
         )
         pbuf[p, me] = part[0:4, :]
 
-        def p_start(j, _):
-            pltpu.make_async_remote_copy(
-                pbuf.at[p, me], pbuf.at[p, me], p_send.at[p, j], p_recv.at[p, me],
-                device_id=((me + j) % NP, z), device_id_type=MESH,
-            ).start()
-            return 0
-
-        def p_wait(j, _):
-            other = (me + j) % NP
-            pltpu.make_async_remote_copy(
-                pbuf.at[p, other], pbuf.at[p, other], p_send.at[p, j], p_recv.at[p, other],
-                device_id=(other, z), device_id_type=MESH,
-            ).wait_recv()
-            return 0
-
-        lax.fori_loop(1, NP, p_start, 0)
+        def p_copy(i, o, slot):
+            return copy(pbuf.at[p, slot], pbuf.at[p, slot], p_send.at[p, i], p_recv.at[p, slot], (o, z))
+
+        over_p(lambda i, o: p_copy(i, o, me).start())
         if p == 1:
             for i in range(3):
                 for d in range(3):
                     rt[3 * i + d : 3 * i + d + 1, :] = rotation[i][d]
                 rt[9 + i : 10 + i, :] = centroid[i]
             columns = jnp.transpose(rt[...])[0:F, :]
-            shifted = [
-                fa[at : at + F, :] - columns[:, 9 + i : 10 + i] for i, at in enumerate((0, 2 * F, F))
-            ]
+            shifted = [frames_ref[i] - columns[:, 9 + i : 10 + i] for i in range(3)]
             for d in range(3):
                 al[d] = sum(columns[:, 3 * i + d : 3 * i + d + 1] * shifted[i] for i in range(3))
-        lax.fori_loop(1, NP, p_wait, 0)
+        over_p(lambda i, o: p_copy(i, o, o).wait_recv())
         summed = pbuf[p, 0]
         for i in range(1, NP):
             summed = summed + pbuf[p, i]
@@ -185,19 +168,26 @@
     for d in range(3):
         col[c, k, :, d * A : (d + 1) * A] = (al[d] - mean_now[d : d + 1, :]).astype(jnp.bfloat16)
 
-    @pl.when(c == z)
+    leg_z = (5 * z + c) % NZ
+    leg_p = (13 * (z + NZ - c)) % NZ
+    seed = (z + 5 * NZ - 5 * c) % NZ
+
+    def leg_1(n):
+        rows = pl.ds(n * Q, Q)
+        return copy(col.at[c, k, rows], mid.at[rows], l_send.at[0, n], l_recv.at[0, n], (me, leg_z))
+
+    def leg_2(n, slot):
+        rows = pl.ds(n * Q, Q)
+        return copy(mid.at[rows], row.at[slot, k, rows], l_send.at[1, n], l_recv.at[1, n], (leg_p * 2 + k, z))
+
+    @pl.when(leg_z != z)
     def _():
-        row[z, k] = col[c, k]
-
-    def copy(src, dst, send, recv, device):
-        return pltpu.make_async_remote_copy(src, dst, send, recv, device_id=device, device_id_type=MESH)
-
-    def swap(slot):
-        return copy(col.at[c, k], row.at[slot, k], swap_send, swap_recv, partner)
-
-    @pl.when(c != z)
+        for n in range(CH):
+            leg_1(n).start()
+
+    @pl.when(leg_z == z)
     def _():
-        swap(c).start()
+        mid[...] = col[c, k]
 
     def chip(oa, ob):
         qa, qb = (pa + oa) % 4, (pb + ob) % 4
@@ -249,23 +239,24 @@
 
     right, left = (me, (z + 1) % NZ), (me, (z + NZ - 1) % NZ)
 
+    def off(offset):
+        return (seed + offset) % NZ
+
     def r_copy(way, step, h, slot):
-        r = row.at[slot, k, h * H : (h + 1) * H]
+        r = row.at[slot, k, h * Q : (h + 1) * Q]
         return copy(r, r, r_send.at[way, step, h], r_recv.at[way, step, h], right if way == 0 else left)
 
     def row_sibling(offset, core):
-        r = row.at[(z + offset) % NZ, core]
+        r = row.at[off(offset), core]
         return copy(r, r, rs_send.at[offset], rs_recv.at[offset], sibling)
 
     def z_step(s, last=False):
-        before, after = (z + NZ - s) % NZ, (z + s) % NZ
-        for h in range(2):
-            r_copy(0, s - 1, h, before).wait_recv()
-            if not last or h == 0:
-                r_copy(0, s, h, before).start()
-            r_copy(1, s - 1, h, after).wait_recv()
-            if not last or h == 1:
-                r_copy(1, s, h, after).start()
+        slots = off(NZ - s), off(s)
+        for h in range(CH):
+            for way in range(2):
+                r_copy(way, s - 1, h, slots[way]).wait_recv()
+                if not last or h // (CH // 2) == way:
+                    r_copy(way, s, h, slots[way]).start()
         row_sibling(NZ - s, k).start()
         row_sibling(s, k).start()
 
@@ -286,33 +277,48 @@
     def z_compute(s):
         row_sibling(s, 1 - k).wait_recv()
         row_sibling(NZ - s, 1 - k).wait_recv()
-        accumulate((z + NZ - s) % NZ, (z + s) % NZ)
+        accumulate(off(NZ - s), off(s))
 
     a_copy(0, c).start()
     a_copy(1, c).start()
     have(0)
     a_copy(0, chip(3, 0)).wait_recv()
     a_copy(2, chip(3, 0)).start()
-    have(3)
     a_copy(1, chip(1, 0)).wait_recv()
     a_copy(3, chip(1, 0)).start()
+
+    for n in range(CH):
+
+        @pl.when(leg_z != z)
+        def _():
+            leg_1(n).wait_recv()
+
+        @pl.when(leg_p != c)
+        def _():
+            leg_2(n, c).start()
+
+    @pl.when(leg_p == c)
+    def _():
+        row[seed, k] = mid[...]
+
+    have(3)
     have(1)
-
-    @pl.when(c != z)
-    def _():
-        swap(z).wait_recv()
-
-    for h in range(2):
-        r_copy(0, 0, h, z).start()
-        r_copy(1, 0, h, z).start()
+    for n in range(CH):
+
+        @pl.when(leg_p != c)
+        def _():
+            leg_2(n, seed).wait_recv()
+
+        for way in range(2):
+            r_copy(way, 0, n, seed).start()
     row_sibling(0, k).start()
     b_pass(0)
     a_copy(2, chip(2, 0)).wait_recv()
     a_copy(3, chip(2, 0)).wait_recv()
     have(2)
     b_pass(3)
+    b_pass(1)
     z_step(1)
-    b_pass(1)
     b_pass(2)
     z_step(2)
     for oa in (0, 3, 1, 2):
@@ -337,25 +343,30 @@
     lax.fori_loop(4, 7, middle, 0)
     z_step(7, last=True)
     lax.fori_loop(6, 8, compute, 0)
-    far = (z + NZ // 2) % NZ
-    r_copy(0, 7, 0, far).wait_recv()
-    r_copy(1, 7, 1, far).wait_recv()
+    far = off(NZ // 2)
+    for h in range(CH):
+        r_copy(h // (CH // 2), NZ // 2 - 1, h, far).wait_recv()
     row_sibling(NZ // 2, k).start()
     row_sibling(0, 1 - k).wait_recv()
     row_sibling(NZ // 2, 1 - k).wait_recv()
-    accumulate(z, far)
-    for d in range(3):
-        cov_ref[d] = acc[d, pl.ds(pl.multiple_of(k * F, F), 192), :] * (1.0 / FRAMES)
-
-    def a_sent(j, _):
-        for p in range(2):
-            copy(zbuf.at[p, z], zbuf.at[p, z], z_send.at[p, j], z_recv.at[p, z], (me, (z + j) % NZ)).wait_send()
-        return 0
-
-    def p_sent(j, _):
-        for p in range(2):
-            copy(pbuf.at[p, me], pbuf.at[p, me], p_send.at[p, j], p_recv.at[p, me], ((me + j) % NP, z)).wait_send()
-        return 0
+    accumulate(seed, far)
+    for i in range(3):
+        for d in range(3):
+            cov_ref[i, d] = acc[i, pl.ds(pl.multiple_of(k * F, F), A // 2), d * A : (d + 1) * A] * (1.0 / FRAMES)
+
+    for p in range(2):
+        over_z(lambda i, o: copy(zbuf.at[p, z], zbuf.at[p, z], z_send.at[p, i], z_recv.at[p, z], (me, o)).wait_send())
+        over_p(lambda i, o: copy(pbuf.at[p, me], pbuf.at[p, me], p_send.at[p, i], p_recv.at[p, me], (o, z)).wait_send())
+
+    for n in range(CH):
+
+        @pl.when(leg_z != z)
+        def _():
+            leg_1(n).wait_send()
+
+        @pl.when(leg_p != c)
+        def _():
+            leg_2(n, seed).wait_send()
 
     def slot_sent(q, _):
         col_sibling(q, k).wait_send()
@@ -369,23 +380,17 @@
 
     def r_sent(s, _):
         for way in range(2):
-            for h in range(2):
-                r_copy(way, s, h, z).wait_send()
-        return 0
-
-    lax.fori_loop(1, NZ, a_sent, 0)
-    lax.fori_loop(1, NP, p_sent, 0)
+            for h in range(CH):
+                r_copy(way, s, h, seed).wait_send()
+        return 0
+
     lax.fori_loop(0, NZ, slot_sent, 0)
     for kind in range(4):
         a_copy(kind, c).wait_send()
     lax.fori_loop(0, 4, b_sent, 0)
     lax.fori_loop(0, NZ // 2 - 1, r_sent, 0)
-    r_copy(0, 7, 0, z).wait_send()
-    r_copy(1, 7, 1, z).wait_send()
-
-    @pl.when(c != z)
-    def _():
-        swap(c).wait_send()
+    for h in range(CH):
+        r_copy(h // (CH // 2), NZ // 2 - 1, h, seed).wait_send()
 
 
 def body(frames, reference_structure):
@@ -394,7 +399,7 @@
     covariance, mean = pl.pallas_call(
         kernel,
         out_shape=(
-            jax.ShapeDtypeStruct((3, A // 2, W), jnp.float32),
+            jax.ShapeDtypeStruct((3, 3, A // 2, A), jnp.float32),
             jax.ShapeDtypeStruct((3, A), jnp.float32),
         ),
         in_specs=[vmem, vmem],
@@ -408,19 +413,20 @@
             pltpu.VMEM((3, F, A), jnp.float32),
             pltpu.VMEM((2, NZ, 8, 2 * F), jnp.float32),
             pltpu.VMEM((2, NP, 4, A), jnp.float32),
+            pltpu.VMEM((F, W), jnp.bfloat16),
             pltpu.VMEM((NZ, 2, F, W), jnp.bfloat16),
             pltpu.VMEM((NZ, 2, F, W), jnp.bfloat16),
             pltpu.VMEM((3, 256, W), jnp.float32),
             dma((2, NZ)), dma((2, NZ)), dma((2, NP)), dma((2, NP)),
             dma((4,)), dma((4,)), dma((4, 4)), dma((4, 4)), dma((NZ,)), dma((NZ,)),
-            dma, dma, dma((2, 8, 2)), dma((2, 8, 2)), dma((NZ,)), dma((NZ,)),
+            dma((2, CH)), dma((2, CH)), dma((2, 8, CH)), dma((2, 8, CH)), dma((NZ,)), dma((NZ,)),
         ],
         compiler_params=pltpu.CompilerParams(
             collective_id=0, has_side_effects=True, vmem_limit_bytes=44 * 1024 * 1024
         ),
         cost_estimate=pl.CostEstimate(flops=3_000_000_000, bytes_accessed=8_000_000, transcendentals=0),
-    )(frames, reference_structure)
-    return covariance.reshape(3, A // 2, 3, A), mean
+    )(jnp.transpose(frames, (1, 0, 2)), reference_structure)
+    return jnp.transpose(covariance, (0, 2, 1, 3)), mean
 
 
 def solution(mesh):

time: 126 us -> 106 us (0.84)
  Pallas kernels: 121 us -> 101 us
    pallas_call x1, Pallas kernels: 121 us -> 101 us  [body(): pl.pallas_call(kernel, out_shape=(jax.ShapeDtypeStruct((3, 3, A // 2, A),...]
    reshape x1 -> x0, local copies, waits for them, and re-layouts: 1.72 us -> none  [body(): return (covariance.reshape(3, A // 2, 3, A), mean)]
    unnamed x4 -> x6, local copies, waits for them, and re-layouts: 2.45 us -> 3.74 us
where the time goes in v2:
time: 106 us
  Pallas kernels  101 us (95%)
  local copies, waits for them, and re-layouts  3.74 us (4%)
    pallas_call x1, Pallas kernels, body(): pl.pallas_call(kernel, out_shape=(jax.ShapeDtypeStruct((3, 3, A // 2, A),...  101 us
    unnamed x6, local copies, waits for them, and re-layouts  3.74 us

profile of v2, /device:TPU:1, one launch (start us, length us, event | category | flops | bytes accessed | tf_op | source)
XLA Modules:
  0.0 105.8 jit_solution(15098327927914215216)
XLA Ops:
  0.6 0.0 copy-start
  0.6 1.0 copy-done
  1.6 0.0 copy-start.1
  1.6 0.7 copy-done.1
  2.3 101.4 %shard_map.41 = (f32[3,3,192,384]{3,2,1,0:T(8,128)S(1)}, f32[3,384]{1,0:T(4,128)S(1)}) custom-call(f32[3,64,384]{2,1,0:T(8,128)S(1)} %bitcast.3, f32[3,384]{1,0:T(4,128)S(1)} %copy-done.1), custom_call_target="tpu_custom_call" | custom-call | flops 3000000000 | bytes 8000000 | tf_op jit(solution)/shard_map/pallas_call | solution.py:399
  103.7 1.5 %copy.6 = f32[3,192,3,384]{3,1,2,0:T(8,128)} copy(f32[3,192,3,384]{3,1,2,0:T(8,128)S(1)} %bitcast.2) | data formatting | bytes 5308416
  105.2 0.6 copy.7
Async XLA Ops:
  0.6 1.0 copy-start
  1.6 0.7 copy-start.1

commit v3 on v2

--- a/solution.py
+++ b/solution.py
@@ -44,8 +44,8 @@
 
 
 def kernel(
-    frames_ref, ref_ref, cov_ref, mean_ref,
-    fa, aug, w, tile, rt, al, zbuf, pbuf, mid, col, row, acc,
+    frames_in, ref_in, cov_ref, mean_ref,
+    frames_ref, ref_ref, fa, aug, w, tile, rt, al, zbuf, pbuf, col, row, acc, in_sem,
     z_send, z_recv, p_send, p_recv,
     a_send, a_recv, b_send, b_recv, cs_send, cs_recv,
     l_send, l_recv, r_send, r_recv, rs_send, rs_recv,
@@ -84,10 +84,26 @@
         lax.fori_loop(0, 20, turn, 0)
         lax.fori_loop(21, NP, turn, 0)
 
+    get_frames = pltpu.make_async_copy(frames_in, frames_ref, in_sem.at[0])
+    get_ref = pltpu.make_async_copy(ref_in, ref_ref, in_sem.at[1])
+    get_frames.start()
+    get_ref.start()
+
+    leg_z = (7 * z + c + 8 * k) % NZ
+    seeds = (z + 9 * c) % NZ
+    seed = (seeds + 8 * k) % NZ
+    moves = jnp.logical_or(z != c, leg_z != z)
+
     barrier = pltpu.get_barrier_semaphore()
     over_z(lambda i, o: pl.semaphore_signal(barrier, inc=1, device_id=(me, o), device_id_type=MESH))
     over_p(lambda i, o: pl.semaphore_signal(barrier, inc=1, device_id=(o, z), device_id_type=MESH))
 
+    @pl.when(moves)
+    def _():
+        pl.semaphore_signal(barrier, inc=1, device_id=(seed * 2 + k, c), device_id_type=MESH)
+
+    get_frames.wait()
+    get_ref.wait()
     fa[0:F, :] = frames_ref[0]
     fa[F : 2 * F, :] = frames_ref[2]
     fa[2 * F : 3 * F, :] = frames_ref[1]
@@ -116,7 +132,7 @@
         aug[12:15, :] = mean_now
         zbuf[p, z] = local_sums()
         if p == 0:
-            pl.semaphore_wait(barrier, NZ + NP - 2)
+            pl.semaphore_wait(barrier, NZ + NP - 2 + jnp.where(moves, 1, 0))
 
         def z_copy(i, o, slot):
             return copy(zbuf.at[p, slot], zbuf.at[p, slot], z_send.at[p, i], z_recv.at[p, slot], (me, o))
@@ -168,26 +184,20 @@
     for d in range(3):
         col[c, k, :, d * A : (d + 1) * A] = (al[d] - mean_now[d : d + 1, :]).astype(jnp.bfloat16)
 
-    leg_z = (5 * z + c) % NZ
-    leg_p = (13 * (z + NZ - c)) % NZ
-    seed = (z + 5 * NZ - 5 * c) % NZ
-
-    def leg_1(n):
+    def leg(n, slot):
         rows = pl.ds(n * Q, Q)
-        return copy(col.at[c, k, rows], mid.at[rows], l_send.at[0, n], l_recv.at[0, n], (me, leg_z))
-
-    def leg_2(n, slot):
-        rows = pl.ds(n * Q, Q)
-        return copy(mid.at[rows], row.at[slot, k, rows], l_send.at[1, n], l_recv.at[1, n], (leg_p * 2 + k, z))
-
-    @pl.when(leg_z != z)
+        return copy(
+            col.at[c, k, rows], row.at[slot, k, rows], l_send.at[n], l_recv.at[n], (z * 2 + k, leg_z)
+        )
+
+    @pl.when(moves)
     def _():
         for n in range(CH):
-            leg_1(n).start()
-
-    @pl.when(leg_z == z)
+            leg(n, c).start()
+
+    @pl.when(jnp.logical_not(moves))
     def _():
-        mid[...] = col[c, k]
+        row[seed, k] = col[c, k]
 
     def chip(oa, ob):
         qa, qb = (pa + oa) % 4, (pb + ob) % 4
@@ -247,7 +257,7 @@
         return copy(r, r, r_send.at[way, step, h], r_recv.at[way, step, h], right if way == 0 else left)
 
     def row_sibling(offset, core):
-        r = row.at[off(offset), core]
+        r = row.at[(seeds + 8 * core + offset) % NZ, core]
         return copy(r, r, rs_send.at[offset], rs_recv.at[offset], sibling)
 
     def z_step(s, last=False):
@@ -260,16 +270,22 @@
         row_sibling(NZ - s, k).start()
         row_sibling(s, k).start()
 
-    def accumulate(one, two):
-        def component(d, _):
-            lanes = pl.ds(pl.multiple_of(d * A + k * 128, 128), 256)
-            lhs = jnp.concatenate(
-                [row[one, 0, :, lanes], row[one, 1, :, lanes], row[two, 0, :, lanes], row[two, 1, :, lanes]], axis=0
-            )
-            rhs = jnp.concatenate([col[one, 0], col[one, 1], col[two, 0], col[two, 1]], axis=0)
-            acc[d] += lax.dot_general(
+    def accumulate(one, two, last=False):
+        pieces = [((seeds + 8 * core + o) % NZ, core) for o in (one, two) for core in range(2)]
+
+        def component(i, _):
+            lanes = pl.ds(pl.multiple_of(i * A + k * 128, 128), 256)
+            lhs = jnp.concatenate([row[q, core, :, lanes] for q, core in pieces], axis=0)
+            rhs = jnp.concatenate([col[q, core] for q, core in pieces], axis=0)
+            total = acc[i] + lax.dot_general(
                 lhs, rhs, (((0,), (0,)), ((), ())), preferred_element_type=jnp.float32
             )
+            if not last:
+                acc[i] = total
+                return 0
+            kept = jnp.where(k == 0, total[0 : A // 2], total[F : F + A // 2]) * (1.0 / FRAMES)
+            for d in range(3):
+                cov_ref[i, d] = kept[:, d * A : (d + 1) * A]
             return 0
 
         lax.fori_loop(0, 3, component, 0)
@@ -277,7 +293,7 @@
     def z_compute(s):
         row_sibling(s, 1 - k).wait_recv()
         row_sibling(NZ - s, 1 - k).wait_recv()
-        accumulate(off(NZ - s), off(s))
+        accumulate(NZ - s, s)
 
     a_copy(0, c).start()
     a_copy(1, c).start()
@@ -287,27 +303,13 @@
     a_copy(1, chip(1, 0)).wait_recv()
     a_copy(3, chip(1, 0)).start()
 
-    for n in range(CH):
-
-        @pl.when(leg_z != z)
-        def _():
-            leg_1(n).wait_recv()
-
-        @pl.when(leg_p != c)
-        def _():
-            leg_2(n, c).start()
-
-    @pl.when(leg_p == c)
-    def _():
-        row[seed, k] = mid[...]
-
     have(3)
     have(1)
     for n in range(CH):
 
-        @pl.when(leg_p != c)
+        @pl.when(moves)
         def _():
-            leg_2(n, seed).wait_recv()
+            leg(n, seed).wait_recv()
 
         for way in range(2):
             r_copy(way, 0, n, seed).start()
@@ -349,10 +351,7 @@
     row_sibling(NZ // 2, k).start()
     row_sibling(0, 1 - k).wait_recv()
     row_sibling(NZ // 2, 1 - k).wait_recv()
-    accumulate(seed, far)
-    for i in range(3):
-        for d in range(3):
-            cov_ref[i, d] = acc[i, pl.ds(pl.multiple_of(k * F, F), A // 2), d * A : (d + 1) * A] * (1.0 / FRAMES)
+    accumulate(0, NZ // 2, last=True)
 
     for p in range(2):
         over_z(lambda i, o: copy(zbuf.at[p, z], zbuf.at[p, z], z_send.at[p, i], z_recv.at[p, z], (me, o)).wait_send())
@@ -360,13 +359,9 @@
 
     for n in range(CH):
 
-        @pl.when(leg_z != z)
+        @pl.when(moves)
         def _():
-            leg_1(n).wait_send()
-
-        @pl.when(leg_p != c)
-        def _():
-            leg_2(n, seed).wait_send()
+            leg(n, seed).wait_send()
 
     def slot_sent(q, _):
         col_sibling(q, k).wait_send()
@@ -396,15 +391,18 @@
 def body(frames, reference_structure):
     dma = pltpu.SemaphoreType.DMA
     vmem = pl.BlockSpec(memory_space=pltpu.VMEM)
+    hbm = pl.BlockSpec(memory_space=pltpu.HBM)
     covariance, mean = pl.pallas_call(
         kernel,
         out_shape=(
             jax.ShapeDtypeStruct((3, 3, A // 2, A), jnp.float32),
             jax.ShapeDtypeStruct((3, A), jnp.float32),
         ),
-        in_specs=[vmem, vmem],
+        in_specs=[hbm, hbm],
         out_specs=(vmem, vmem),
         scratch_shapes=[
+            pltpu.VMEM((3, F, A), jnp.float32),
+            pltpu.VMEM((3, A), jnp.float32),
             pltpu.VMEM((4 * F, A), jnp.float32),
             pltpu.VMEM((16, A), jnp.float32),
             pltpu.VMEM((8, 4 * F), jnp.float32),
@@ -413,13 +411,13 @@
             pltpu.VMEM((3, F, A), jnp.float32),
             pltpu.VMEM((2, NZ, 8, 2 * F), jnp.float32),
             pltpu.VMEM((2, NP, 4, A), jnp.float32),
-            pltpu.VMEM((F, W), jnp.bfloat16),
             pltpu.VMEM((NZ, 2, F, W), jnp.bfloat16),
             pltpu.VMEM((NZ, 2, F, W), jnp.bfloat16),
             pltpu.VMEM((3, 256, W), jnp.float32),
+            dma((2,)),
             dma((2, NZ)), dma((2, NZ)), dma((2, NP)), dma((2, NP)),
             dma((4,)), dma((4,)), dma((4, 4)), dma((4, 4)), dma((NZ,)), dma((NZ,)),
-            dma((2, CH)), dma((2, CH)), dma((2, 8, CH)), dma((2, 8, CH)), dma((NZ,)), dma((NZ,)),
+            dma((CH,)), dma((CH,)), dma((2, 8, CH)), dma((2, 8, CH)), dma((NZ,)), dma((NZ,)),
         ],
         compiler_params=pltpu.CompilerParams(
             collective_id=0, has_side_effects=True, vmem_limit_bytes=44 * 1024 * 1024

time: 106 us -> 104 us (0.981)
  Pallas kernels: 101 us -> 99.2 us
    pallas_call x1, Pallas kernels: 101 us -> 99.2 us  [body(): pl.pallas_call(kernel, out_shape=(jax.ShapeDtypeStruct((3, 3, A // 2, A),...]
where the time goes in v3:
time: 104 us
  Pallas kernels  99.2 us (95%)
  local copies, waits for them, and re-layouts  3.74 us (4%)
    pallas_call x1, Pallas kernels, body(): pl.pallas_call(kernel, out_shape=(jax.ShapeDtypeStruct((3, 3, A // 2, A),...  99.2 us
    unnamed x6, local copies, waits for them, and re-layouts  3.74 us

profile of v3, /device:TPU:1, one launch (start us, length us, event | category | flops | bytes accessed | tf_op | source)
XLA Modules:
  0.0 103.6 jit_solution(9224204780573846667)
XLA Ops:
  0.6 0.0 copy-start
  0.6 1.0 copy-done
  1.6 0.0 copy-start.1
  1.6 0.7 copy-done.1
  2.3 99.2 %shard_map.41 = (f32[3,3,192,384]{3,2,1,0:T(8,128)S(1)}, f32[3,384]{1,0:T(4,128)S(1)}) custom-call(f32[3,64,384]{2,1,0:T(8,128)S(1)} %bitcast.3, f32[3,384]{1,0:T(4,128)S(1)} %copy-done.1), custom_call_target="tpu_custom_call" | custom-call | flops 3000000000 | bytes 8000000 | tf_op jit(solution)/shard_map/pallas_call | solution.py:395
  101.5 1.5 %copy.6 = f32[3,192,3,384]{3,1,2,0:T(8,128)} copy(f32[3,192,3,384]{3,1,2,0:T(8,128)S(1)} %bitcast.2) | data formatting | bytes 5308416
  103.0 0.6 copy.7
Async XLA Ops:
  0.6 1.0 copy-start
  1.6 0.7 copy-start.1

commit v4 on v3

--- a/solution.py
+++ b/solution.py
@@ -63,6 +63,9 @@
     def copy(src, dst, send, recv, device):
         return pltpu.make_async_remote_copy(src, dst, send, recv, device_id=device, device_id_type=MESH)
 
+    def all_of(sized, semaphore):
+        pltpu.make_async_copy(sized, sized, semaphore).wait()
+
     def z_other(i):
         return (z + 8 + ((i + 1) // 2) * (2 * (i % 2) - 1)) % NZ
 
@@ -134,11 +137,11 @@
         if p == 0:
             pl.semaphore_wait(barrier, NZ + NP - 2 + jnp.where(moves, 1, 0))
 
-        def z_copy(i, o, slot):
-            return copy(zbuf.at[p, slot], zbuf.at[p, slot], z_send.at[p, i], z_recv.at[p, slot], (me, o))
-
-        over_z(lambda i, o: z_copy(i, o, z).start())
-        over_z(lambda i, o: z_copy(i, o, o).wait_recv())
+        def z_copy(o, slot):
+            return copy(zbuf.at[p, slot], zbuf.at[p, slot], z_send.at[p], z_recv.at[p], (me, o))
+
+        over_z(lambda i, o: z_copy(o, z).start())
+        all_of(zbuf.at[p, 0 : NZ - 1], z_recv.at[p])
         total = zbuf[p, 0]
         for i in range(1, NZ):
             total = total + zbuf[p, i]
@@ -161,10 +164,10 @@
         )
         pbuf[p, me] = part[0:4, :]
 
-        def p_copy(i, o, slot):
-            return copy(pbuf.at[p, slot], pbuf.at[p, slot], p_send.at[p, i], p_recv.at[p, slot], (o, z))
-
-        over_p(lambda i, o: p_copy(i, o, me).start())
+        def p_copy(o, slot):
+            return copy(pbuf.at[p, slot], pbuf.at[p, slot], p_send.at[p], p_recv.at[p], (o, z))
+
+        over_p(lambda i, o: p_copy(o, me).start())
         if p == 1:
             for i in range(3):
                 for d in range(3):
@@ -174,7 +177,7 @@
             shifted = [frames_ref[i] - columns[:, 9 + i : 10 + i] for i in range(3)]
             for d in range(3):
                 al[d] = sum(columns[:, 3 * i + d : 3 * i + d + 1] * shifted[i] for i in range(3))
-        over_p(lambda i, o: p_copy(i, o, o).wait_recv())
+        all_of(pbuf.at[p, 0 : NP - 1], p_recv.at[p])
         summed = pbuf[p, 0]
         for i in range(1, NP):
             summed = summed + pbuf[p, i]
@@ -182,12 +185,12 @@
 
     mean_ref[...] = mean_now
     for d in range(3):
-        col[c, k, :, d * A : (d + 1) * A] = (al[d] - mean_now[d : d + 1, :]).astype(jnp.bfloat16)
+        col[me, :, d * A : (d + 1) * A] = (al[d] - mean_now[d : d + 1, :]).astype(jnp.bfloat16)
 
     def leg(n, slot):
         rows = pl.ds(n * Q, Q)
         return copy(
-            col.at[c, k, rows], row.at[slot, k, rows], l_send.at[n], l_recv.at[n], (z * 2 + k, leg_z)
+            col.at[me, rows], row.at[slot * 2 + k, rows], l_send, l_recv.at[n], (z * 2 + k, leg_z)
         )
 
     @pl.when(moves)
@@ -197,7 +200,7 @@
 
     @pl.when(jnp.logical_not(moves))
     def _():
-        row[seed, k] = col[c, k]
+        row[seed * 2 + k] = col[me]
 
     def chip(oa, ob):
         qa, qb = (pa + oa) % 4, (pb + ob) % 4
@@ -208,23 +211,23 @@
 
     def part_of(slot, half):
         if half is None:
-            return col.at[slot, k]
-        return col.at[slot, k, half * H : (half + 1) * H]
+            return col.at[slot * 2 + k]
+        return col.at[slot * 2 + k, half * H : (half + 1) * H]
 
     HALF = (None, None, 0, 1)
     TOWARD = (1, 3, 1, 3)
 
     def a_copy(kind, slot):
         r = part_of(slot, HALF[kind])
-        return copy(r, r, a_send.at[kind], a_recv.at[kind], at(TOWARD[kind], 0))
+        return copy(r, r, a_send, a_recv.at[kind], at(TOWARD[kind], 0))
 
     def b_copy(oa, kind, slot):
         r = part_of(slot, HALF[kind])
-        return copy(r, r, b_send.at[oa, kind], b_recv.at[oa, kind], at(0, TOWARD[kind]))
+        return copy(r, r, b_send, b_recv.at[oa, kind], at(0, TOWARD[kind]))
 
     def col_sibling(slot, core):
-        r = col.at[slot, core]
-        return copy(r, r, cs_send.at[slot], cs_recv.at[slot], sibling)
+        r = col.at[slot * 2 + core]
+        return copy(r, r, cs_send, cs_recv, sibling)
 
     def have(oa):
         slot = chip(oa, 0)
@@ -253,12 +256,12 @@
         return (seed + offset) % NZ
 
     def r_copy(way, step, h, slot):
-        r = row.at[slot, k, h * Q : (h + 1) * Q]
-        return copy(r, r, r_send.at[way, step, h], r_recv.at[way, step, h], right if way == 0 else left)
+        r = row.at[slot * 2 + k, h * Q : (h + 1) * Q]
+        return copy(r, r, r_send, r_recv.at[way, step, h], right if way == 0 else left)
 
     def row_sibling(offset, core):
-        r = row.at[(seeds + 8 * core + offset) % NZ, core]
-        return copy(r, r, rs_send.at[offset], rs_recv.at[offset], sibling)
+        r = row.at[(seeds + 8 * core + offset) % NZ * 2 + core]
+        return copy(r, r, rs_send, rs_recv.at[offset], sibling)
 
     def z_step(s, last=False):
         slots = off(NZ - s), off(s)
@@ -271,12 +274,12 @@
         row_sibling(s, k).start()
 
     def accumulate(one, two, last=False):
-        pieces = [((seeds + 8 * core + o) % NZ, core) for o in (one, two) for core in range(2)]
+        pieces = [(seeds + 8 * core + o) % NZ * 2 + core for o in (one, two) for core in range(2)]
 
         def component(i, _):
             lanes = pl.ds(pl.multiple_of(i * A + k * 128, 128), 256)
-            lhs = jnp.concatenate([row[q, core, :, lanes] for q, core in pieces], axis=0)
-            rhs = jnp.concatenate([col[q, core] for q, core in pieces], axis=0)
+            lhs = jnp.concatenate([row[q, :, lanes] for q in pieces], axis=0)
+            rhs = jnp.concatenate([col[q] for q in pieces], axis=0)
             total = acc[i] + lax.dot_general(
                 lhs, rhs, (((0,), (0,)), ((), ())), preferred_element_type=jnp.float32
             )
@@ -326,10 +329,6 @@
     for oa in (0, 3, 1, 2):
         b_end(oa)
 
-    def col_wait(q, _):
-        col_sibling(q, 1 - k).wait_recv()
-        return 0
-
     def compute(s, _):
         z_compute(s)
         return 0
@@ -340,52 +339,31 @@
         return 0
 
     z_step(3)
-    lax.fori_loop(0, NZ, col_wait, 0)
+    all_of(col.at[0:NZ], cs_recv)
     lax.fori_loop(1, 3, compute, 0)
     lax.fori_loop(4, 7, middle, 0)
     z_step(7, last=True)
     lax.fori_loop(6, 8, compute, 0)
     far = off(NZ // 2)
+    for p in range(2):
+        all_of(zbuf.at[p, 0 : NZ - 1], z_send.at[p])
+        all_of(pbuf.at[p, 0 : NP - 1], p_send.at[p])
+
+    @pl.when(moves)
+    def _():
+        all_of(col.at[0], l_send)
+
+    all_of(col.at[0:3], a_send)
+    all_of(col.at[0:12], b_send)
+    all_of(col.at[0:NZ], cs_send)
     for h in range(CH):
         r_copy(h // (CH // 2), NZ // 2 - 1, h, far).wait_recv()
     row_sibling(NZ // 2, k).start()
     row_sibling(0, 1 - k).wait_recv()
     row_sibling(NZ // 2, 1 - k).wait_recv()
     accumulate(0, NZ // 2, last=True)
-
-    for p in range(2):
-        over_z(lambda i, o: copy(zbuf.at[p, z], zbuf.at[p, z], z_send.at[p, i], z_recv.at[p, z], (me, o)).wait_send())
-        over_p(lambda i, o: copy(pbuf.at[p, me], pbuf.at[p, me], p_send.at[p, i], p_recv.at[p, me], (o, z)).wait_send())
-
-    for n in range(CH):
-
-        @pl.when(moves)
-        def _():
-            leg(n, seed).wait_send()
-
-    def slot_sent(q, _):
-        col_sibling(q, k).wait_send()
-        row_sibling(q, k).wait_send()
-        return 0
-
-    def b_sent(oa, _):
-        for kind in range(4):
-            b_copy(oa, kind, c).wait_send()
-        return 0
-
-    def r_sent(s, _):
-        for way in range(2):
-            for h in range(CH):
-                r_copy(way, s, h, seed).wait_send()
-        return 0
-
-    lax.fori_loop(0, NZ, slot_sent, 0)
-    for kind in range(4):
-        a_copy(kind, c).wait_send()
-    lax.fori_loop(0, 4, b_sent, 0)
-    lax.fori_loop(0, NZ // 2 - 1, r_sent, 0)
-    for h in range(CH):
-        r_copy(h // (CH // 2), NZ // 2 - 1, h, seed).wait_send()
+    all_of(row.at[0 : NZ - 1], r_send)
+    all_of(row.at[0:NZ], rs_send)
 
 
 def body(frames, reference_structure):
@@ -411,13 +389,13 @@
             pltpu.VMEM((3, F, A), jnp.float32),
             pltpu.VMEM((2, NZ, 8, 2 * F), jnp.float32),
             pltpu.VMEM((2, NP, 4, A), jnp.float32),
-            pltpu.VMEM((NZ, 2, F, W), jnp.bfloat16),
-            pltpu.VMEM((NZ, 2, F, W), jnp.bfloat16),
+            pltpu.VMEM((NP, F, W), jnp.bfloat16),
+            pltpu.VMEM((NP, F, W), jnp.bfloat16),
             pltpu.VMEM((3, 256, W), jnp.float32),
             dma((2,)),
-            dma((2, NZ)), dma((2, NZ)), dma((2, NP)), dma((2, NP)),
-            dma((4,)), dma((4,)), dma((4, 4)), dma((4, 4)), dma((NZ,)), dma((NZ,)),
-            dma((CH,)), dma((CH,)), dma((2, 8, CH)), dma((2, 8, CH)), dma((NZ,)), dma((NZ,)),
+            dma((2,)), dma((2,)), dma((2,)), dma((2,)),
+            dma, dma((4,)), dma, dma((4, 4)), dma, dma,
+            dma, dma((CH,)), dma, dma((2, 8, CH)), dma, dma((NZ,)),
         ],
         compiler_params=pltpu.CompilerParams(
             collective_id=0, has_side_effects=True, vmem_limit_bytes=44 * 1024 * 1024

time: 104 us -> 99.4 us (0.956)
  Pallas kernels: 99.2 us -> 94.8 us
    pallas_call x1, Pallas kernels: 99.2 us -> 94.8 us  [body(): pl.pallas_call(kernel, out_shape=(jax.ShapeDtypeStruct((3, 3, A // 2, A),...]
where the time goes in v4:
time: 99.4 us; the launch traced here: 99.2 us
  Pallas kernels  94.8 us (95%)
  local copies, waits for them, and re-layouts  3.74 us (4%)
    pallas_call x1, Pallas kernels, body(): pl.pallas_call(kernel, out_shape=(jax.ShapeDtypeStruct((3, 3, A // 2, A),...  94.8 us
    unnamed x6, local copies, waits for them, and re-layouts  3.74 us

profile of v4, /device:TPU:1, one launch (start us, length us, event | category | flops | bytes accessed | tf_op | source)
XLA Modules:
  0.0 99.2 jit_solution(15605993926183367770)
XLA Ops:
  0.6 0.0 copy-start
  0.6 1.0 copy-done
  1.6 0.0 copy-start.1
  1.6 0.7 copy-done.1
  2.3 94.8 %shard_map.41 = (f32[3,3,192,384]{3,2,1,0:T(8,128)S(1)}, f32[3,384]{1,0:T(4,128)S(1)}) custom-call(f32[3,64,384]{2,1,0:T(8,128)S(1)} %bitcast.3, f32[3,384]{1,0:T(4,128)S(1)} %copy-done.1), custom_call_target="tpu_custom_call" | custom-call | flops 3000000000 | bytes 8000000 | tf_op jit(solution)/shard_map/pallas_call | solution.py:373
  97.1 1.5 %copy.6 = f32[3,192,3,384]{3,1,2,0:T(8,128)} copy(f32[3,192,3,384]{3,1,2,0:T(8,128)S(1)} %bitcast.2) | data formatting | bytes 5308416
  98.6 0.6 copy.7
Async XLA Ops:
  0.6 1.0 copy-start
  1.6 0.7 copy-start.1

commit v5 on v4

--- a/solution.py
+++ b/solution.py
@@ -98,12 +98,13 @@
     moves = jnp.logical_or(z != c, leg_z != z)
 
     barrier = pltpu.get_barrier_semaphore()
-    over_z(lambda i, o: pl.semaphore_signal(barrier, inc=1, device_id=(me, o), device_id_type=MESH))
-    over_p(lambda i, o: pl.semaphore_signal(barrier, inc=1, device_id=(o, z), device_id_type=MESH))
 
     @pl.when(moves)
     def _():
         pl.semaphore_signal(barrier, inc=1, device_id=(seed * 2 + k, c), device_id_type=MESH)
+
+    over_z(lambda i, o: pl.semaphore_signal(barrier, inc=1, device_id=(me, o), device_id_type=MESH))
+    over_p(lambda i, o: pl.semaphore_signal(barrier, inc=1, device_id=(o, z), device_id_type=MESH))
 
     get_frames.wait()
     get_ref.wait()
@@ -193,10 +194,14 @@
             col.at[me, rows], row.at[slot * 2 + k, rows], l_send, l_recv.at[n], (z * 2 + k, leg_z)
         )
 
-    @pl.when(moves)
-    def _():
+    hops = (leg_z - z + NZ) % NZ
+    near = jnp.logical_or(hops <= 3, hops >= NZ - 3)
+
+    def leave():
         for n in range(CH):
             leg(n, c).start()
+
+    pl.when(jnp.logical_and(moves, jnp.logical_not(near)))(leave)
 
     @pl.when(jnp.logical_not(moves))
     def _():
@@ -263,40 +268,54 @@
         r = row.at[(seeds + 8 * core + offset) % NZ * 2 + core]
         return copy(r, r, rs_send, rs_recv.at[offset], sibling)
 
-    def z_step(s, last=False):
+    def z_step(s, last=False, between=None):
         slots = off(NZ - s), off(s)
         for h in range(CH):
             for way in range(2):
                 r_copy(way, s - 1, h, slots[way]).wait_recv()
                 if not last or h // (CH // 2) == way:
                     r_copy(way, s, h, slots[way]).start()
+            if between is not None and h < 3:
+                between(h)
         row_sibling(NZ - s, k).start()
         row_sibling(s, k).start()
 
-    def accumulate(one, two, last=False):
+    def product(one, two, i):
         pieces = [(seeds + 8 * core + o) % NZ * 2 + core for o in (one, two) for core in range(2)]
-
-        def component(i, _):
-            lanes = pl.ds(pl.multiple_of(i * A + k * 128, 128), 256)
-            lhs = jnp.concatenate([row[q, :, lanes] for q in pieces], axis=0)
-            rhs = jnp.concatenate([col[q] for q in pieces], axis=0)
-            total = acc[i] + lax.dot_general(
-                lhs, rhs, (((0,), (0,)), ((), ())), preferred_element_type=jnp.float32
-            )
-            if not last:
-                acc[i] = total
-                return 0
-            kept = jnp.where(k == 0, total[0 : A // 2], total[F : F + A // 2]) * (1.0 / FRAMES)
-            for d in range(3):
-                cov_ref[i, d] = kept[:, d * A : (d + 1) * A]
-            return 0
-
-        lax.fori_loop(0, 3, component, 0)
-
-    def z_compute(s):
+        lanes = pl.ds(pl.multiple_of(i * A + k * 128, 128), 256)
+        lhs = jnp.concatenate([row[q, :, lanes] for q in pieces], axis=0)
+        rhs = jnp.concatenate([col[q] for q in pieces], axis=0)
+        return acc[i] + lax.dot_general(
+            lhs, rhs, (((0,), (0,)), ((), ())), preferred_element_type=jnp.float32
+        )
+
+    def add(s, i):
+        acc[i] = product(NZ - s, s, i)
+
+    def arrived(s):
         row_sibling(s, 1 - k).wait_recv()
         row_sibling(NZ - s, 1 - k).wait_recv()
-        accumulate(NZ - s, s)
+
+    def compute(s, _):
+        arrived(s)
+
+        def component(i, _):
+            add(s, i)
+            return 0
+
+        return lax.fori_loop(0, 3, component, 0)
+
+    def finish(i, _):
+        total = product(0, NZ // 2, i)
+        kept = jnp.where(k == 0, total[0 : A // 2], total[F : F + A // 2]) * (1.0 / FRAMES)
+        for d in range(3):
+            cov_ref[i, d] = kept[:, d * A : (d + 1) * A]
+        return 0
+
+    def step_and_add(s, last=False):
+        arrived(s - 2)
+        z_step(s, last, lambda i: add(s - 2, i))
+        return 0
 
     a_copy(0, c).start()
     a_copy(1, c).start()
@@ -305,7 +324,7 @@
     a_copy(2, chip(3, 0)).start()
     a_copy(1, chip(1, 0)).wait_recv()
     a_copy(3, chip(1, 0)).start()
-
+    pl.when(jnp.logical_and(moves, near))(leave)
     have(3)
     have(1)
     for n in range(CH):
@@ -329,20 +348,11 @@
     for oa in (0, 3, 1, 2):
         b_end(oa)
 
-    def compute(s, _):
-        z_compute(s)
-        return 0
-
-    def middle(s, _):
-        z_step(s)
-        z_compute(s - 1)
-        return 0
-
     z_step(3)
     all_of(col.at[0:NZ], cs_recv)
-    lax.fori_loop(1, 3, compute, 0)
-    lax.fori_loop(4, 7, middle, 0)
-    z_step(7, last=True)
+    compute(1, 0)
+    lax.fori_loop(4, 7, lambda s, _: step_and_add(s), 0)
+    step_and_add(7, last=True)
     lax.fori_loop(6, 8, compute, 0)
     far = off(NZ // 2)
     for p in range(2):
@@ -361,7 +371,7 @@
     row_sibling(NZ // 2, k).start()
     row_sibling(0, 1 - k).wait_recv()
     row_sibling(NZ // 2, 1 - k).wait_recv()
-    accumulate(0, NZ // 2, last=True)
+    lax.fori_loop(0, 3, finish, 0)
     all_of(row.at[0 : NZ - 1], r_send)
     all_of(row.at[0:NZ], rs_send)
 
@@ -369,7 +379,7 @@
 def body(frames, reference_structure):
     dma = pltpu.SemaphoreType.DMA
     vmem = pl.BlockSpec(memory_space=pltpu.VMEM)
-    hbm = pl.BlockSpec(memory_space=pltpu.HBM)
+    hbm = pl.BlockSpec(memory_space=pl.ANY)
     covariance, mean = pl.pallas_call(
         kernel,
         out_shape=(

time: 99.4 us -> 97.3 us (0.979)
  Pallas kernels: 94.8 us -> 92.7 us
    pallas_call x1, Pallas kernels: 94.8 us -> 92.7 us  [body(): pl.pallas_call(kernel, out_shape=(jax.ShapeDtypeStruct((3, 3, A // 2, A),...]
where the time goes in v5:
time: 97.3 us; the launch traced here: 97.1 us
  Pallas kernels  92.7 us (95%)
  local copies, waits for them, and re-layouts  3.74 us (4%)
    pallas_call x1, Pallas kernels, body(): pl.pallas_call(kernel, out_shape=(jax.ShapeDtypeStruct((3, 3, A // 2, A),...  92.7 us
    unnamed x6, local copies, waits for them, and re-layouts  3.74 us

profile of v5, /device:TPU:1, one launch (start us, length us, event | category | flops | bytes accessed | tf_op | source)
XLA Modules:
  0.0 97.1 jit_solution(6231901906842976946)
XLA Ops:
  0.6 0.0 copy-start
  0.6 1.0 copy-done
  1.6 0.0 copy-start.1
  1.6 0.7 copy-done.1
  2.3 92.7 %shard_map.41 = (f32[3,3,192,384]{3,2,1,0:T(8,128)S(1)}, f32[3,384]{1,0:T(4,128)S(1)}) custom-call(f32[3,64,384]{2,1,0:T(8,128)S(1)} %bitcast.3, f32[3,384]{1,0:T(4,128)S(1)} %copy-done.1), custom_call_target="tpu_custom_call" | custom-call | flops 3000000000 | bytes 8000000 | tf_op jit(solution)/shard_map/pallas_call | solution.py:383
  95.0 1.5 %copy.6 = f32[3,192,3,384]{3,1,2,0:T(8,128)} copy(f32[3,192,3,384]{3,1,2,0:T(8,128)S(1)} %bitcast.2) | data formatting | bytes 5308416
  96.5 0.6 copy.7
Async XLA Ops:
  0.6 1.0 copy-start
  1.6 0.7 copy-start.1

commit v6 on v5

--- a/solution.py
+++ b/solution.py
@@ -99,10 +99,6 @@
 
     barrier = pltpu.get_barrier_semaphore()
 
-    @pl.when(moves)
-    def _():
-        pl.semaphore_signal(barrier, inc=1, device_id=(seed * 2 + k, c), device_id_type=MESH)
-
     over_z(lambda i, o: pl.semaphore_signal(barrier, inc=1, device_id=(me, o), device_id_type=MESH))
     over_p(lambda i, o: pl.semaphore_signal(barrier, inc=1, device_id=(o, z), device_id_type=MESH))
 
@@ -136,7 +132,7 @@
         aug[12:15, :] = mean_now
         zbuf[p, z] = local_sums()
         if p == 0:
-            pl.semaphore_wait(barrier, NZ + NP - 2 + jnp.where(moves, 1, 0))
+            pl.semaphore_wait(barrier, NZ + NP - 2)
 
         def z_copy(o, slot):
             return copy(zbuf.at[p, slot], zbuf.at[p, slot], z_send.at[p], z_recv.at[p], (me, o))

time: 97.3 us -> 97.1 us (level)
  no operation moved by 1% of the time
where the time goes in v6:
time: 97.1 us; the launch traced here: 96.9 us
  Pallas kernels  92.5 us (95%)
  local copies, waits for them, and re-layouts  3.74 us (4%)
    pallas_call x1, Pallas kernels, body(): pl.pallas_call(kernel, out_shape=(jax.ShapeDtypeStruct((3, 3, A // 2, A),...  92.5 us
    unnamed x6, local copies, waits for them, and re-layouts  3.74 us

profile of v6, /device:TPU:1, one launch (start us, length us, event | category | flops | bytes accessed | tf_op | source)
XLA Modules:
  0.0 96.9 jit_solution(11050133423670363917)
XLA Ops:
  0.6 0.0 copy-start
  0.6 1.0 copy-done
  1.6 0.0 copy-start.1
  1.6 0.7 copy-done.1
  2.3 92.5 %shard_map.41 = (f32[3,3,192,384]{3,2,1,0:T(8,128)S(1)}, f32[3,384]{1,0:T(4,128)S(1)}) custom-call(f32[3,64,384]{2,1,0:T(8,128)S(1)} %bitcast.3, f32[3,384]{1,0:T(4,128)S(1)} %copy-done.1), custom_call_target="tpu_custom_call" | custom-call | flops 3000000000 | bytes 8000000 | tf_op jit(solution)/shard_map/pallas_call | solution.py:379
  94.8 1.5 %copy.6 = f32[3,192,3,384]{3,1,2,0:T(8,128)} copy(f32[3,192,3,384]{3,1,2,0:T(8,128)S(1)} %bitcast.2) | data formatting | bytes 5308416
  96.3 0.6 copy.7
Async XLA Ops:
  0.6 1.0 copy-start
  1.6 0.7 copy-start.1

commit v7 on v5

--- a/solution.py
+++ b/solution.py
@@ -280,8 +280,8 @@
         row_sibling(NZ - s, k).start()
         row_sibling(s, k).start()
 
-    def product(one, two, i):
-        pieces = [(seeds + 8 * core + o) % NZ * 2 + core for o in (one, two) for core in range(2)]
+    def product(offsets, i):
+        pieces = [(seeds + 8 * core + o) % NZ * 2 + core for o in offsets for core in range(2)]
         lanes = pl.ds(pl.multiple_of(i * A + k * 128, 128), 256)
         lhs = jnp.concatenate([row[q, :, lanes] for q in pieces], axis=0)
         rhs = jnp.concatenate([col[q] for q in pieces], axis=0)
@@ -290,7 +290,7 @@
         )
 
     def add(s, i):
-        acc[i] = product(NZ - s, s, i)
+        acc[i] = product((NZ - s, s), i)
 
     def arrived(s):
         row_sibling(s, 1 - k).wait_recv()
@@ -305,8 +305,12 @@
 
         return lax.fori_loop(0, 3, component, 0)
 
+    def add_seeds(i, _):
+        acc[i] = product((0,), i)
+        return 0
+
     def finish(i, _):
-        total = product(0, NZ // 2, i)
+        total = product((NZ // 2,), i)
         kept = jnp.where(k == 0, total[0 : A // 2], total[F : F + A // 2]) * (1.0 / FRAMES)
         for d in range(3):
             cov_ref[i, d] = kept[:, d * A : (d + 1) * A]
@@ -353,7 +357,10 @@
     compute(1, 0)
     lax.fori_loop(4, 7, lambda s, _: step_and_add(s), 0)
     step_and_add(7, last=True)
-    lax.fori_loop(6, 8, compute, 0)
+    lax.fori_loop(6, 7, compute, 0)
+    row_sibling(0, 1 - k).wait_recv()
+    lax.fori_loop(0, 3, add_seeds, 0)
+    compute(7, 0)
     far = off(NZ // 2)
     for p in range(2):
         all_of(zbuf.at[p, 0 : NZ - 1], z_send.at[p])
@@ -369,7 +376,6 @@
     for h in range(CH):
         r_copy(h // (CH // 2), NZ // 2 - 1, h, far).wait_recv()
     row_sibling(NZ // 2, k).start()
-    row_sibling(0, 1 - k).wait_recv()
     row_sibling(NZ // 2, 1 - k).wait_recv()
     lax.fori_loop(0, 3, finish, 0)
     all_of(row.at[0 : NZ - 1], r_send)

time: 97.3 us -> 98 us (level)
  no operation moved by 1% of the time
where the time goes in v7:
time: 98 us; the launch traced here: 97.8 us
  Pallas kernels  93.4 us (95%)
  local copies, waits for them, and re-layouts  3.74 us (4%)
    pallas_call x1, Pallas kernels, body(): pl.pallas_call(kernel, out_shape=(jax.ShapeDtypeStruct((3, 3, A // 2, A),...  93.4 us
    unnamed x6, local copies, waits for them, and re-layouts  3.74 us

profile of v7, /device:TPU:1, one launch (start us, length us, event | category | flops | bytes accessed | tf_op | source)
XLA Modules:
  0.0 97.8 jit_solution(13364257947021216284)
XLA Ops:
  0.6 0.0 copy-start
  0.6 1.0 copy-done
  1.6 0.0 copy-start.1
  1.6 0.7 copy-done.1
  2.3 93.4 %shard_map.41 = (f32[3,3,192,384]{3,2,1,0:T(8,128)S(1)}, f32[3,384]{1,0:T(4,128)S(1)}) custom-call(f32[3,64,384]{2,1,0:T(8,128)S(1)} %bitcast.3, f32[3,384]{1,0:T(4,128)S(1)} %copy-done.1), custom_call_target="tpu_custom_call" | custom-call | flops 3000000000 | bytes 8000000 | tf_op jit(solution)/shard_map/pallas_call | solution.py:389
  95.7 1.5 %copy.6 = f32[3,192,3,384]{3,1,2,0:T(8,128)} copy(f32[3,192,3,384]{3,1,2,0:T(8,128)S(1)} %bitcast.2) | data formatting | bytes 5308416
  97.2 0.6 copy.7
Async XLA Ops:
  0.6 1.0 copy-start
  1.6 0.7 copy-start.1
